TPU v7x, 32 devices: a whole 2x2x4 slice. The times are simulated.
32 devices in a mesh: row: 8 (over z, y), col: 4 (over x, core).
Axes of the slice: x: 2, y: 2, z: 4, core: 2. Of those that a mesh axis runs over, the one named last changes fastest.
Arguments:
- points: float32 [32, 8192], P(None, ('row', 'col')), may hold values from -6 to 6
- candidates: float32 [32, 2048], P(None, ('row', 'col')), may hold values from -6 to 6
- length_scales: float32 [32], replicated, may hold values from 1.5 to 4
- signal_var: float32 [1], replicated, may hold values from 0.5 to 2
- noise_var: float32 [1], replicated, may hold values from 0.1 to 1
- cand_prior: float32 [2048], P(('row', 'col')), may hold values from -6 to 6
- weights: float32 [16, 8192], P(None, ('row', 'col')), may hold values from -6 to 6
- residual: float32 [16, 8192], P(None, ('row', 'col')), may hold values from -300 to 300, as said below
- direction: float32 [16, 8192], P(None, ('row', 'col')), may hold values from -300 to 300, as said below
Outputs:
- weights_new: float32 [16, 8192], P(None, ('row', 'col'))
- residual_new: float32 [16, 8192], P(None, ('row', 'col'))
- direction_new: float32 [16, 8192], P(None, ('row', 'col'))
- cand_fit: float32 [16, 2048], P(None, ('row', 'col'))
Inputs may be any that keep to these rules, and one draw needn't show every extreme that they name: `residual`: real values. `direction`: real values.
All inputs are finite; a program needn't handle non-finite values.
Results may differ from a plain program's by a relative error of at most 0.011.
Values may be sent and summed in bfloat16 or wider, within the bound.
A program may use at most 64 MiB of HBM per device.

v0:
```python
import math

import jax
import jax.numpy as jnp
from jax import lax
from jax.sharding import PartitionSpec as P

root_five = math.sqrt(5.0)
contract_first = (((0,), (0,)), ((), ()))
contract_last = (((1,), (1,)), ((), ()))


def square_norms(scaled):
    return jnp.sum(jnp.square(scaled.astype(jnp.float32)), axis=0)


def matern_block(row_pts, row_sq, col_pts, col_sq, signal_scalar):
    inner_prod = lax.dot_general(
        row_pts, col_pts, contract_first, preferred_element_type=jnp.float32
    )
    dist_sq = jnp.maximum(row_sq[:, None] + col_sq[None, :] - 2.0 * inner_prod, 0.0)
    distance = jnp.sqrt(dist_sq)
    kern_vals = (
        signal_scalar
        * (1.0 + root_five * distance + 5.0 / 3.0 * dist_sq)
        * jnp.exp(-root_five * distance)
    )
    return kern_vals.astype(jnp.bfloat16)


def kernel_apply(running, row_pts, row_sq, col_pts, col_sq, vectors, signal_scalar):
    row_count = row_pts.shape[1]
    width_all = col_pts.shape[1]
    block_len = math.gcd(width_all, max(256, 1048576 // row_count))
    num_blocks = width_all // block_len

    def one_block(total, pieces):
        pts_blk, sq_blk, vec_blk = pieces
        kern_vals = matern_block(row_pts, row_sq, pts_blk, sq_blk, signal_scalar)
        return (
            total
            + lax.dot_general(
                vec_blk, kern_vals, contract_last, preferred_element_type=jnp.float32
            ),
            None,
        )

    if num_blocks == 1:
        return one_block(running, (col_pts, col_sq, vectors))[0]
    feature_count = col_pts.shape[0]
    pts_blocks = col_pts.reshape(feature_count, num_blocks, block_len).transpose(1, 0, 2)
    sq_blocks = col_sq.reshape(num_blocks, block_len)
    vec_blocks = vectors.reshape(vectors.shape[0], num_blocks, block_len).transpose(1, 0, 2)
    result, ignored = lax.scan(one_block, running, (pts_blocks, sq_blocks, vec_blocks))
    return result


def per_device(
    points,
    candidates,
    length_scales,
    signal_var,
    noise_var,
    cand_prior,
    weights,
    residual,
    direction,
):
    scaled = (points / length_scales[:, None]).astype(jnp.bfloat16)
    cand_scaled = (candidates / length_scales[:, None]).astype(jnp.bfloat16)
    signal_scalar = signal_var[0]
    dir_low = direction.astype(jnp.bfloat16)
    col_total = direction.shape[0]
    norm_now = lax.psum(jnp.sum(residual * residual, axis=1), ("row", "col"))
    row_pts, row_cands = (
        lax.all_gather(scaled, "col", axis=1, tiled=True),
        lax.all_gather(cand_scaled, "col", axis=1, tiled=True),
    )
    col_pts = lax.all_gather(scaled, "row", axis=1, tiled=True)
    row_sq = square_norms(row_pts)
    col_sq = square_norms(col_pts)
    cand_sq = square_norms(row_cands)
    start_rows = jnp.zeros((col_total, row_pts.shape[1]), jnp.float32)
    pts_piece = col_pts
    sq_piece = col_sq
    partial_rows = kernel_apply(
        start_rows,
        row_pts,
        row_sq,
        pts_piece,
        sq_piece,
        lax.all_gather(dir_low, "row", axis=1, tiled=True),
        signal_scalar,
    )
    kernel_out = lax.psum_scatter(partial_rows, "col", scatter_dimension=1, tiled=True)
    image_vec = kernel_out + noise_var[0] * direction
    curvature = lax.psum(jnp.sum(direction * image_vec, axis=1), ("row", "col"))
    step_len = norm_now / curvature
    weights_new = weights + step_len[:, None] * direction
    residual_new = residual - step_len[:, None] * image_vec
    norm_next = lax.psum(jnp.sum(residual_new * residual_new, axis=1), ("row", "col"))
    direction_new = residual_new + (norm_next / norm_now)[:, None] * direction
    w_low = weights_new.astype(jnp.bfloat16)
    start_cands = jnp.zeros((col_total, row_cands.shape[1]), jnp.float32)
    pts_piece = col_pts
    sq_piece = col_sq
    partial_fit = kernel_apply(
        start_cands,
        row_cands,
        cand_sq,
        pts_piece,
        sq_piece,
        lax.all_gather(w_low, "row", axis=1, tiled=True),
        signal_scalar,
    )
    fitted = lax.psum_scatter(partial_fit, "col", scatter_dimension=1, tiled=True)
    cand_fit = cand_prior[None, :] + fitted
    return (weights_new, residual_new, direction_new, cand_fit)


def solution(mesh):
    placed = (
        P(None, ("row", "col")),
        P(None, ("row", "col")),
        P(),
        P(),
        P(),
        P(("row", "col")),
        P(None, ("row", "col")),
        P(None, ("row", "col")),
        P(None, ("row", "col")),
    )
    return jax.shard_map(
        per_device,
        mesh=mesh,
        in_specs=placed,
        out_specs=(
            P(None, ("row", "col")),
            P(None, ("row", "col")),
            P(None, ("row", "col")),
            P(None, ("row", "col")),
        ),
        check_vma=False,
    )
```

profile of v0, /device:TPU:0, one launch (start us, length us, event | category | flops | bytes accessed | tf_op | source)
XLA Modules:
  0.0 249.9 jit_solution(10068960057504232759)
XLA Ops:
  7.2 0.0 reduce-scatter.5.cloned.1.call-start
  7.2 0.8 divide_convert_fusion
  8.1 32.3 %all_gather.17 = bf16[32,2048]{1,0:T(8,128)(2,1)S(1)} all-gather(bf16[32,256]{1,0:T(8,128)(2,1)S(1)} %divide_convert_fusion), channel_id=1, replica_groups=mesh['row'=8,'col'=4] {'row'}, dimensions={1}, use_global_device_ids=true | all-gather | bytes 147456 | tf_op jit(solution)/shard_map/all_gather | solution.py:79
  40.4 5.2 %all_gather.16 = bf16[32,1024]{1,0:T(8,128)(2,1)S(1)} all-gather(bf16[32,256]{1,0:T(8,128)(2,1)S(1)} %divide_convert_fusion), channel_id=1, replica_groups=mesh['row'=8,'col'=4] {'col'}, dimensions={1}, use_global_device_ids=true | all-gather | bytes 81920 | tf_op jit(solution)/shard_map/all_gather | solution.py:76
  45.7 0.0 copy-start
  45.7 0.7 copy-done
  46.4 30.5 %all_gather.15 = bf16[16,2048]{1,0:T(8,128)(2,1)S(1)} all-gather(bf16[16,256]{1,0:T(8,128)(2,1)S(1)} %convert_element_type.27), channel_id=1, replica_groups=mesh['row'=8,'col'=4] {'row'}, dimensions={1}, use_global_device_ids=true | all-gather | bytes 73728 | tf_op jit(solution)/shard_map/all_gather | solution.py:92
  76.9 0.0 copy-start.4
  76.9 0.0 copy-start.6
  77.0 0.0 copy-start.3
  77.0 7.7 %while.11 = (s32[]{:T(128)}, f32[16,1024]{1,0:T(8,128)S(1)}, bf16[2,16,1024]{2,1,0:T(8,128)(2,1)S(1)}, f32[]{:T(128)}, f32[1024]{0:T(1024)S(1)}, /*index=5*/f32[...) while((s32[]{:T(128)}, f32[16,1024]{1,0:T(8,128)S(1)}, ...), condition=%wide.region_5.6_spmd.clone, body=%wide.region_4.0_spmd.clone.sunk | while | flops 113278976 | bytes 312947 | solution.py:54
  77.0 3.8 %fusion.49 = f32[16,1024]{1,0:T(8,128)S(1)} fusion(bf16[32,1024]{1,0:T(8,128)(2,1)S(1)} %get-tuple-element.190, f32[1024]{0:T(1024)S(1)} %bitcast.57, f32[1024]{0:T(1024)S(1)} %get-tuple-element.187, f32[]{:T(128)} %get-tuple-element.186, f32[16,1024]{1,0:T(8,128)S(1)} %get-tuple-element.174, bf16[2,32,1024]{2,1,0:T(8,128)(2,1)S(1)} %get-tuple-element.189, ...), kind=kOutput, calls=%fused_computation.4.clone.1 | convolution fusion | flops 113278976 | bytes 304641 | tf_op jit(solution)/shard_map/while/body/eval_jaxpr/dot_general | solution.py:42
  80.9 3.8 %fusion.49 = f32[16,1024]{1,0:T(8,128)S(1)} fusion(bf16[32,1024]{1,0:T(8,128)(2,1)S(1)} %get-tuple-element.190, f32[1024]{0:T(1024)S(1)} %bitcast.57, f32[1024]{0:T(1024)S(1)} %get-tuple-element.187, f32[]{:T(128)} %get-tuple-element.186, f32[16,1024]{1,0:T(8,128)S(1)} %get-tuple-element.174, bf16[2,32,1024]{2,1,0:T(8,128)(2,1)S(1)} %get-tuple-element.189, ...), kind=kOutput, calls=%fused_computation.4.clone.1 | convolution fusion | flops 113278976 | bytes 304641 | tf_op jit(solution)/shard_map/while/body/eval_jaxpr/dot_general | solution.py:42
  84.7 0.6 copy-done.1
  85.3 0.0 reduce-scatter.5.cloned.1.call-update
  85.3 0.0 reduce-scatter.7.cloned.1.call-start
  85.4 0.1 fusion.30
  85.5 0.1 multiply_reduce_fusion.5
  86.3 5.2 %all-gather = bf16[4,64,32]{1,2,0:T(8,128)(2,1)S(1)} all-gather(bf16[1,64,32]{1,2,0:T(8,128)(2,1)S(1)} %fusion.30), channel_id=1, replica_groups=mesh['row'=8,'col'=4] {'col'}, dimensions={0}, use_global_device_ids=true | all-gather | bytes 20480 | tf_op jit(solution)/shard_map/all_gather | solution.py:77
  91.5 0.1 reshape.28
  91.6 14.2 %reduce-scatter.5.cloned.1.call-done = f32[16,256]{1,0:T(8,128)} async-done(((f32[16,1024]{1,0:T(8,128)}), f32[16,256]{1,0:T(8,128)}) %reduce-scatter.5.cloned.1.call-update) | async-done | bytes 16400 | tf_op jit(solution)/shard_map/reduce_scatter | solution.py:95
  105.8 0.8 multiply_reduce_fusion.4
  107.3 39.4 %all-reduce = (f32[16]{0:T(128)S(1)}, f32[16]{0:T(128)S(1)}) all-reduce(f32[16]{0:T(128)S(1)} %multiply_reduce_fusion.5, f32[16]{0:T(128)S(1)} %multiply_reduce_fusion.4), channel_id=1, replica_groups=mesh['row'=8,'col'=4] {'row','col'}, use_global_device_ids=true, to_apply=%region_1.0 | all-reduce | flops 32 | bytes 256 | tf_op jit(solution)/shard_map/psum | solution.py:74
  146.7 1.5 multiply_reduce_fusion.3
  148.2 41.0 %psum.23 = f32[16]{0:T(128)S(1)} all-reduce(f32[16]{0:T(128)S(1)} %get-tuple-element.110), channel_id=1, replica_groups=mesh['row'=8,'col'=4] {'row','col'}, use_global_device_ids=true, to_apply=%region_10.11 | all-reduce | flops 16 | bytes 128 | tf_op jit(solution)/shard_map/psum | solution.py:101
  189.2 30.5 %all_gather.18 = bf16[16,2048]{1,0:T(8,128)(2,1)S(1)} all-gather(bf16[16,256]{1,0:T(8,128)(2,1)S(1)} %get-tuple-element.112), channel_id=1, replica_groups=mesh['row'=8,'col'=4] {'row'}, dimensions={1}, use_global_device_ids=true | all-gather | bytes 73728 | tf_op jit(solution)/shard_map/all_gather | solution.py:113
  219.7 2.3 fusion.20
  222.1 0.0 reduce-scatter.7.cloned.1.call-update
  222.1 0.7 multiply_add_fusion
  222.8 18.8 %reduce-scatter.7.cloned.1.call-done = f32[64,16]{1,0:T(8,128)} async-done(((f32[256,16]{1,0:T(8,128)}), f32[64,16]{1,0:T(8,128)}) %reduce-scatter.7.cloned.1.call-update) | async-done | bytes 4112
  241.6 0.8 copy.21
  242.4 0.6 broadcast_add_fusion
  (24 shorter events, 0.2 us)
Async XLA Ops:
  7.2 98.7 %reduce-scatter.5.cloned.1.call-start = ((), (), s32[]{:S(2)}) async-start(), calls=%async_computation.2 | async-start | bytes 81920 | tf_op jit(solution)/shard_map/reduce_scatter | solution.py:95
  45.7 0.7 copy-start
  76.9 8.5 %copy-start.4 = (f32[32,64]{1,0:T(8,128)S(1)}, f32[32,64]{1,0:T(8,128)}, u32[]{:S(2)}) copy-start(f32[32,64]{1,0:T(8,128)} %param.12) | copy-start | bytes 24580
  76.9 8.5 %copy-start.6 = (f32[32]{0:T(128)S(1)}, f32[32]{0:T(128)}, u32[]{:S(2)}) copy-start(f32[32]{0:T(128)} %param.13) | copy-start | bytes 388
  77.0 8.5 %copy-start.3 = (f32[16,256]{1,0:T(8,128)S(1)}, f32[16,256]{1,0:T(8,128)}, u32[]{:S(2)}) copy-start(f32[16,256]{1,0:T(8,128)} %param.18) | copy-start | bytes 49156
  84.7 0.6 copy-start.1
  85.3 61.4 %copy-start.5 = (f32[16,256]{1,0:T(8,128)S(1)}, f32[16,256]{1,0:T(8,128)}, u32[]{:S(2)}) copy-start(f32[16,256]{1,0:T(8,128)} %param.17) | copy-start | bytes 49156
  85.3 156.2 %reduce-scatter.7.cloned.1.call-start = ((), (), s32[]{:S(2)}) async-start(), calls=%async_computation.3 | async-start | bytes 163840
  148.2 73.9 %copy-start.2 = (f32[16,256]{1,0:T(8,128)}, f32[16,256]{1,0:T(8,128)S(1)}, u32[]{:S(2)}) copy-start(f32[16,256]{1,0:T(8,128)S(1)} %get-tuple-element.111) | copy-start | bytes 49156
  222.1 20.3 %copy-start.7 = (f32[64]{0:T(128)S(1)}, f32[64]{0:T(128)}, u32[]{:S(2)}) copy-start(f32[64]{0:T(128)} %param.16) | copy-start | bytes 772
Sparse Core Ops, SparseCore 0:
  85.4 20.3 reduce-scatter.4
  222.2 19.3 reduce-scatter.6
where the time goes:
time: 251 us; the launch traced here: 250 us
  blocking collectives  184 us (73%)
  waiting for transfers between devices  33.1 us (13%)
  between operations  15.5 us (6%)
  matrix products  9.97 us (4%)
  other arithmetic  4.77 us (2%)
    psum x1, blocking collectives, per_device(): lax.psum(jnp.sum(residual_new * residual_new, axis=1), ('row', 'col'))  41 us
    psum x1, blocking collectives, per_device(): norm_now = lax.psum(jnp.sum(residual * residual, axis=1), ('row', 'col'))  39.4 us
    all_gather x1, blocking collectives, per_device(): col_pts = lax.all_gather(scaled, 'row', axis=1, tiled=True)  32.3 us
    all_gather x1, blocking collectives, per_device(): lax.all_gather(w_low, 'row', axis=1, tiled=True)  30.5 us
    all_gather x1, blocking collectives, per_device(): lax.all_gather(dir_low, 'row', axis=1, tiled=True)  30.5 us
    unnamed x3, waiting for transfers between devices  18.8 us
    reduce_scatter x1, waiting for transfers between devices, per_device(): lax.psum_scatter(partial_rows, 'col', scatter_dimension=1, tiled=True)  14.2 us
    dot_general x2, matrix products, one_block(): lax.dot_general(vec_blk, kern_vals, contract_last, preferred_element_type...  7.63 us
  transfers between devices with their start and end apart: 2, of which 2 were waited for; matrix products, arithmetic and copies ran while one was open for 0% of the time, Pallas kernels for 0%

commit v1 on v0

v1 whole, which is shorter than its diff:
```python
import functools
import math

import jax
import jax.numpy as jnp
from jax import lax
from jax.experimental import pallas as pl
from jax.experimental.pallas import tpu as pltpu
from jax.sharding import PartitionSpec as P

MESH = pl.DeviceIdType.MESH
f32 = jnp.float32
bf16 = jnp.bfloat16
LOG2E = math.log2(math.e)


def flip(index, step, size):
    total, bit = 0, 1
    while bit < size:
        total = total + bit * lax.rem(lax.div(index, bit) + lax.div(step, bit), 2)
        bit *= 2
    return total


def split3(x):
    hi = x.astype(bf16).astype(f32)
    mid = (x - hi).astype(bf16).astype(f32)
    return hi, mid, x - hi - mid


def norm_tail(sq, ones_first, one):
    n = sq.shape[1]
    row = lax.broadcasted_iota(jnp.int32, (16, n), 0)
    base = 3 if ones_first else 0
    const = 0 if ones_first else 3
    out = jnp.where((row >= const) & (row < const + 3), f32(one), f32(0))
    for k, piece in enumerate(split3(sq)):
        out = jnp.where(row == base + k, jnp.broadcast_to(piece, (16, n)), out)
    return out.astype(bf16)


def row_operand(a):
    sq = 5.0 * jnp.sum(a * a, axis=0, keepdims=True)
    return jnp.concatenate(
        [(-8.0 * a).astype(bf16), (-2.0 * a).astype(bf16), norm_tail(sq, False, 5.0)], axis=0
    )


def col_operand(b):
    wide = b.astype(f32)
    sq = jnp.sum(wide * wide, axis=0, keepdims=True)
    return jnp.concatenate([b, b, norm_tail(sq, True, 1.0)], axis=0)


def matern(v):
    v = jnp.maximum(v, 1e-30)
    u = v * lax.rsqrt(v)
    return ((1.0 + u + v * f32(1.0 / 3.0)) * jnp.exp2(u * f32(-LOG2E))).astype(bf16)


def kernel(
    R, C,
    pts_hbm, cand_hbm, ls_hbm, sig_ref, noise_ref, prior_hbm, w_hbm, r_hbm, d_hbm,
    wn_ref, rn_ref, dn_ref, cf_ref,
    pts_v, cand_v, ls_v, prior_v, w_v, r_v, d_v,
    b_all, a_pts, a_cand, a_op, part, part_in, cpart, cout, cin, st_a, st_b,
    in_sem, b_send, b_recv, a_send, a_recv, c_send, c_recv,
    p_send, p_recv, q_send, q_recv, s_send, s_recv, t_send, t_recv,
):
    row = lax.axis_index("row")
    col = lax.axis_index("col")
    L = pts_v.shape[1]
    Q = cand_v.shape[1]

    loads = [
        pltpu.make_async_copy(src, dst, in_sem.at[i])
        for i, (src, dst) in enumerate(
            [(ls_hbm, ls_v), (pts_hbm, pts_v), (cand_hbm, cand_v), (d_hbm, d_v),
             (w_hbm, w_v), (r_hbm, r_v), (prior_hbm, prior_v)]
        )
    ]
    for copy in loads:
        copy.start()

    barrier = pltpu.get_barrier_semaphore()
    for k in range(1, C):
        pl.semaphore_signal(barrier, inc=1, device_id=(row, flip(col, k, C)), device_id_type=MESH)
    for k in range(1, R):
        pl.semaphore_signal(barrier, inc=1, device_id=(flip(row, k, R), col), device_id_type=MESH)

    def col_copy(k, src, dst, send, recv):
        peer = flip(col, k, C)
        return pltpu.make_async_remote_copy(
            src_ref=src, dst_ref=dst.at[col], send_sem=send.at[k], recv_sem=recv.at[col],
            device_id=(row, peer), device_id_type=MESH,
        )

    def col_arrive(k, dst, recv):
        peer = flip(col, k, C)
        pltpu.make_async_remote_copy(
            src_ref=dst.at[peer], dst_ref=dst.at[peer], send_sem=recv.at[peer],
            recv_sem=recv.at[peer], device_id=(row, peer), device_id_type=MESH,
        ).wait_recv()

    def row_copy(k, src, dst, send, recv):
        peer = flip(row, k, R)
        return pltpu.make_async_remote_copy(
            src_ref=src, dst_ref=dst.at[row], send_sem=send.at[k], recv_sem=recv.at[row],
            device_id=(peer, col), device_id_type=MESH,
        )

    def row_arrive(k, dst, recv):
        peer = flip(row, k, R)
        pltpu.make_async_remote_copy(
            src_ref=dst.at[peer], dst_ref=dst.at[peer], send_sem=recv.at[peer],
            recv_sem=recv.at[peer], device_id=(peer, col), device_id_type=MESH,
        ).wait_recv()

    for copy in loads[:3]:
        copy.wait()
    eye = lax.broadcasted_iota(jnp.int32, (32, 32), 0) == lax.broadcasted_iota(jnp.int32, (32, 32), 1)
    scale = jnp.sum(jnp.where(eye, jnp.broadcast_to(ls_v[...], (32, 32)), 0.0), axis=1, keepdims=True)
    scaled = (pts_v[...] / scale).astype(bf16)
    b_all[row, 0:32, :] = scaled
    a_pts[col] = scaled
    a_cand[col] = (cand_v[...] / scale).astype(bf16)
    for copy in loads[3:]:
        copy.wait()
    b_all[row, 32:48, :] = d_v[...].astype(bf16)
    b_all[row, 48:64, :] = w_v[...].astype(bf16)

    pl.semaphore_wait(barrier, C - 1 + R - 1)
    sends = []
    for k in range(1, C):
        sends.append(col_copy(k, a_pts.at[col], a_pts, a_send, a_recv))
        sends[-1].start()
        sends.append(col_copy(k, a_cand.at[col], a_cand, c_send, c_recv))
        sends[-1].start()
    for k in range(1, R):
        sends.append(row_copy(k, b_all.at[row], b_all, b_send, b_recv))
        sends[-1].start()

    part[...] = jnp.zeros_like(part)
    cpart[...] = jnp.zeros_like(cpart)

    for k in range(1, C):
        col_arrive(k, a_pts, a_recv)
        col_arrive(k, a_cand, c_recv)
    for k in range(C):
        a_op[k] = row_operand(a_pts[k].astype(f32))
    per_tile = L // Q
    tiles = C // per_tile
    for t in range(tiles):
        wide = None
        for k in range(per_tile):
            place = (
                lax.broadcasted_iota(jnp.int32, (Q, L), 1)
                == lax.broadcasted_iota(jnp.int32, (Q, L), 0) + k * Q
            ).astype(f32).astype(bf16)
            term = jnp.dot(a_cand[t * per_tile + k], place, preferred_element_type=f32)
            wide = term if wide is None else wide + term
        a_op[C + t] = row_operand(wide)

    def chunk(src):
        b_op = col_operand(b_all[src, 0:32, :])
        d_low = b_all[src, 32:48, :]
        both = b_all[src, 32:64, :]
        for t in range(C + tiles):
            v = lax.dot_general(
                b_op, a_op[t], (((0,), (0,)), ((), ())), preferred_element_type=f32
            )
            kern = matern(v)
            if t < C:
                part[t] += jnp.dot(d_low, kern, preferred_element_type=f32)
            else:
                cpart[t - C] += jnp.dot(both, kern, preferred_element_type=f32)

    chunk(row)

    def step(k, carry):
        row_arrive(k, b_all, b_recv)
        chunk(flip(row, k, R))
        return carry

    lax.fori_loop(1, R, step, 0)

    for k in range(1, C):
        sends.append(col_copy(k, part.at[flip(col, k, C)], part_in, p_send, p_recv))
        sends[-1].start()
    for t in range(tiles):
        for k in range(per_tile):
            cout[t * per_tile + k] = cpart[t, :, k * Q:(k + 1) * Q]
    for k in range(1, C):
        sends.append(col_copy(k, cout.at[flip(col, k, C)], cin, q_send, q_recv))
        sends[-1].start()

    signal = sig_ref[0]
    d = d_v[...]
    r = r_v[...]
    total = part[col]
    for k in range(1, C):
        col_arrive(k, part_in, p_recv)
        total = total + part_in[flip(col, k, C)]
    image = signal * total + noise_ref[0] * d

    lane = lax.broadcasted_iota(jnp.int32, (16, 128), 1)
    sub = lax.broadcasted_iota(jnp.int32, (16, 128), 0)
    packed = jnp.zeros((16, 128), f32)
    for q, product in enumerate((r * r, d * image, r * image, image * image)):
        value = jnp.sum(product, axis=1, keepdims=True)
        packed = packed + jnp.where(lane == sub + 16 * q, value, 0.0)
    packed = jnp.sum(packed, axis=0, keepdims=True)

    st_a[col] = packed
    for k in range(1, C):
        sends.append(col_copy(k, st_a.at[col], st_a, s_send, s_recv))
        sends[-1].start()
    for k in range(1, C):
        col_arrive(k, st_a, s_recv)
    st_b[row] = jnp.sum(st_a[...], axis=0)
    for k in range(1, R):
        sends.append(row_copy(k, st_b.at[row], st_b, t_send, t_recv))
        sends[-1].start()

    fit = cout[col]
    for k in range(1, C):
        col_arrive(k, cin, q_recv)
        fit = fit + cin[flip(col, k, C)]

    for k in range(1, R):
        row_arrive(k, st_b, t_recv)
    sums = jnp.broadcast_to(jnp.sum(st_b[...], axis=0), (16, 128))

    def column(q):
        return jnp.sum(jnp.where(lane == sub + 16 * q, sums, 0.0), axis=1, keepdims=True)

    norm_now, curvature, cross, image_sq = column(0), column(1), column(2), column(3)
    step_len = norm_now / curvature
    norm_next = jnp.maximum(norm_now - 2.0 * (step_len * cross) + step_len * (step_len * image_sq), 0.0)
    r_new = r - step_len * image
    wn_ref[...] = w_v[...] + step_len * d
    rn_ref[...] = r_new
    dn_ref[...] = r_new + (norm_next / norm_now) * d
    cf_ref[...] = prior_v[...] + signal * (fit[16:32] + step_len * fit[0:16])
    for copy in sends:
        copy.wait_send()


def per_device(R, C, points, candidates, length_scales, signal_var, noise_var, cand_prior, weights, residual, direction):
    F, L = points.shape
    Q = candidates.shape[1]
    cols = weights.shape[0]
    tiles = C * Q // L
    hbm = pl.BlockSpec(memory_space=pl.ANY)
    smem = pl.BlockSpec(memory_space=pltpu.SMEM)
    vmem = pl.BlockSpec(memory_space=pltpu.VMEM)
    dma = pltpu.SemaphoreType.DMA
    state = jax.ShapeDtypeStruct((cols, L), f32)
    return pl.pallas_call(
        functools.partial(kernel, R, C),
        out_shape=(state, state, state, jax.ShapeDtypeStruct((cols, Q), f32)),
        in_specs=[hbm, hbm, hbm, smem, smem, hbm, hbm, hbm, hbm],
        out_specs=(vmem, vmem, vmem, vmem),
        scratch_shapes=[
            pltpu.VMEM((F, L), f32),
            pltpu.VMEM((F, Q), f32),
            pltpu.VMEM((1, F), f32),
            pltpu.VMEM((1, Q), f32),
            pltpu.VMEM((cols, L), f32),
            pltpu.VMEM((cols, L), f32),
            pltpu.VMEM((cols, L), f32),
            pltpu.VMEM((R, F + 2 * cols, L), bf16),
            pltpu.VMEM((C, F, L), bf16),
            pltpu.VMEM((C, F, Q), bf16),
            pltpu.VMEM((C + tiles, 2 * F + 16, L), bf16),
            pltpu.VMEM((C, cols, L), f32),
            pltpu.VMEM((C, cols, L), f32),
            pltpu.VMEM((tiles, 2 * cols, L), f32),
            pltpu.VMEM((C, 2 * cols, Q), f32),
            pltpu.VMEM((C, 2 * cols, Q), f32),
            pltpu.VMEM((C, 1, 128), f32),
            pltpu.VMEM((R, 1, 128), f32),
            dma((7,)),
            dma((R,)), dma((R,)),
            dma((C,)), dma((C,)),
            dma((C,)), dma((C,)),
            dma((C,)), dma((C,)),
            dma((C,)), dma((C,)),
            dma((C,)), dma((C,)),
            dma((R,)), dma((R,)),
        ],
        compiler_params=pltpu.CompilerParams(
            collective_id=0, has_side_effects=True, vmem_limit_bytes=48 * 1024 * 1024
        ),
    )(
        points, candidates, length_scales[None, :], signal_var, noise_var,
        cand_prior[None, :], weights, residual, direction,
    )


def solution(mesh):
    split = P(None, ("row", "col"))
    return jax.shard_map(
        functools.partial(per_device, mesh.shape["row"], mesh.shape["col"]),
        mesh=mesh,
        in_specs=(split, split, P(), P(), P(), P(("row", "col")), split, split, split),
        out_specs=(split, split, split, split),
        check_vma=False,
    )
```

time: 251 us -> 37.4 us (0.15)
  blocking collectives: 184 us -> 0 us
  waiting for transfers between devices: 33.1 us -> 0 us
  Pallas kernels: 0 us -> 28.2 us
  between operations: 15.5 us -> 1.96 us
  matrix products: 9.97 us -> 0 us
  other arithmetic: 4.77 us -> 0 us
  local copies, waits for them, and re-layouts: 2.33 us -> 6.7 us
    all_gather x5 -> x0, blocking collectives: 104 us -> none  [the longest x1 32.3 us: per_device(): col_pts = lax.all_gather(scaled, 'row', axis=1, tiled=True)]
    psum x2 -> x0, blocking collectives: 80.4 us -> none  [the longest x1 41 us: per_device(): lax.psum(jnp.sum(residual_new * residual_new, axis=1), ('row', 'col'))]
    pallas_call x0 -> x1, Pallas kernels: none -> 28.2 us  [per_device(): pl.pallas_call(functools.partial(kernel, R, C), out_shape=(state, state,...]
    unnamed x3 -> x0, waiting for transfers between devices: 18.8 us -> none
    reduce_scatter x1 -> x0, waiting for transfers between devices: 14.2 us -> none  [per_device(): lax.psum_scatter(partial_rows, 'col', scatter_dimension=1, tiled=True)]
    dot_general x2 -> x0, matrix products: 7.63 us -> none  [one_block(): lax.dot_general(vec_blk, kern_vals, contract_last, preferred_element_type...]
    unnamed x19 -> x18, local copies, waits for them, and re-layouts: 2.24 us -> 6.7 us
    reduce_sum x6 -> x0, other arithmetic: 2.55 us -> none  [the longest x1 1.51 us: per_device(): jnp.sum(residual_new * residual_new, axis=1)]
  transfers between devices with their start and end apart: 2 -> 0, of which waited for: 2 -> 0; matrix products, arithmetic and copies ran while one was open for 0% -> 0% of each run, Pallas kernels for 0% -> 0%
where the time goes in v1:
time: 37.4 us; the launch traced here: 36.9 us
  Pallas kernels  28.2 us (75%)
  local copies, waits for them, and re-layouts  6.7 us (18%)
  between operations  1.96 us (5%)
    pallas_call x1, Pallas kernels, per_device(): pl.pallas_call(functools.partial(kernel, R, C), out_shape=(state, state,...  28.2 us
    unnamed x18, local copies, waits for them, and re-layouts  6.7 us

profile of v1, /device:TPU:0, one launch (start us, length us, event | category | flops | bytes accessed | tf_op | source)
XLA Modules:
  0.0 36.9 jit_solution(16158043700840656969)
XLA Ops:
  1.9 0.0 copy-start.5
  1.9 0.0 copy-start.6
  1.9 0.6 %copy-done.5 = f32[32]{0:T(128)S(1)} copy-done((f32[32]{0:T(128)S(1)}, f32[32]{0:T(128)}, u32[]{:S(2)}) %copy-start.5) | copy-done | bytes 152
  2.6 0.0 copy-done.6
  2.6 0.0 copy-start
  2.6 0.8 %copy-done = f32[32,256]{1,0:T(8,128)S(1)} copy-done((f32[32,256]{1,0:T(8,128)S(1)}, f32[32,256]{1,0:T(8,128)}, u32[]{:S(2)}) %copy-start) | copy-done | bytes 32792
  3.4 0.0 copy-start.1
  3.4 0.7 %copy-done.1 = f32[32,64]{1,0:T(8,128)S(1)} copy-done((f32[32,64]{1,0:T(8,128)S(1)}, f32[32,64]{1,0:T(8,128)}, u32[]{:S(2)}) %copy-start.1) | copy-done | bytes 8216
  4.1 0.0 copy-start.2
  4.1 0.7 %copy-done.2 = f32[16,256]{1,0:T(8,128)S(1)} copy-done((f32[16,256]{1,0:T(8,128)S(1)}, f32[16,256]{1,0:T(8,128)}, u32[]{:S(2)}) %copy-start.2) | copy-done | bytes 16408
  4.8 0.0 copy-start.3
  4.8 0.7 %copy-done.3 = f32[16,256]{1,0:T(8,128)S(1)} copy-done((f32[16,256]{1,0:T(8,128)S(1)}, f32[16,256]{1,0:T(8,128)}, u32[]{:S(2)}) %copy-start.3) | copy-done | bytes 16408
  5.5 0.0 copy-start.4
  5.5 0.7 %copy-done.4 = f32[16,256]{1,0:T(8,128)S(1)} copy-done((f32[16,256]{1,0:T(8,128)S(1)}, f32[16,256]{1,0:T(8,128)}, u32[]{:S(2)}) %copy-start.4) | copy-done | bytes 16408
  6.2 28.2 %shard_map.120 = (f32[16,256]{1,0:T(8,128)S(1)}, f32[16,256]{1,0:T(8,128)S(1)}, f32[16,256]{1,0:T(8,128)S(1)}, f32[16,64]{1,0:T(8,128)S(1)}) custom-call(f32[32,256]{1,0:T(8,128)S(1)} %copy-done, f32[32,64]{1,0:T(8,128)S(1)} %copy-done.1, f32[1,32]{1,0:T(1,128)S(1)} %bitcast.2, f32[1]{0:T(128)S(6)} %copy.17.sig_ref, f32[1]{0:T(128)S(6)} %copy.18.noise_ref, ...), custom_call_target="tpu_custom_call" | custom-call | tf_op jit(solution)/shard_map/pallas_call | solution.py:259
  34.5 0.6 %copy.19 = f32[16,256]{1,0:T(8,128)} copy(f32[16,256]{1,0:T(8,128)S(1)} %get-tuple-element.8) | data formatting | bytes 32768
  35.1 0.6 %copy.20 = f32[16,256]{1,0:T(8,128)} copy(f32[16,256]{1,0:T(8,128)S(1)} %get-tuple-element.9) | data formatting | bytes 32768
  35.7 0.6 %copy.21 = f32[16,256]{1,0:T(8,128)} copy(f32[16,256]{1,0:T(8,128)S(1)} %get-tuple-element.10) | data formatting | bytes 32768
  36.3 0.6 %copy.22 = f32[16,64]{1,0:T(8,128)} copy(f32[16,64]{1,0:T(8,128)S(1)} %get-tuple-element.11) | data formatting | bytes 8192
Async XLA Ops:
  1.9 0.7 %copy-start.5 = (f32[32]{0:T(128)S(1)}, f32[32]{0:T(128)}, u32[]{:S(2)}) copy-start(f32[32]{0:T(128)} %param.11) | copy-start | bytes 388
  1.9 0.7 %copy-start.6 = (f32[64]{0:T(128)S(1)}, f32[64]{0:T(128)}, u32[]{:S(2)}) copy-start(f32[64]{0:T(128)} %param.14) | copy-start | bytes 772
  2.6 0.8 %copy-start = (f32[32,256]{1,0:T(8,128)S(1)}, f32[32,256]{1,0:T(8,128)}, u32[]{:S(2)}) copy-start(f32[32,256]{1,0:T(8,128)} %pts_hbm.1) | copy-start | bytes 98308
  3.4 0.7 %copy-start.1 = (f32[32,64]{1,0:T(8,128)S(1)}, f32[32,64]{1,0:T(8,128)}, u32[]{:S(2)}) copy-start(f32[32,64]{1,0:T(8,128)} %cand_hbm.1) | copy-start | bytes 24580
  4.1 0.7 %copy-start.2 = (f32[16,256]{1,0:T(8,128)S(1)}, f32[16,256]{1,0:T(8,128)}, u32[]{:S(2)}) copy-start(f32[16,256]{1,0:T(8,128)} %w_hbm.1) | copy-start | bytes 49156
  4.8 0.7 %copy-start.3 = (f32[16,256]{1,0:T(8,128)S(1)}, f32[16,256]{1,0:T(8,128)}, u32[]{:S(2)}) copy-start(f32[16,256]{1,0:T(8,128)} %r_hbm.1) | copy-start | bytes 49156
  5.5 0.7 %copy-start.4 = (f32[16,256]{1,0:T(8,128)S(1)}, f32[16,256]{1,0:T(8,128)}, u32[]{:S(2)}) copy-start(f32[16,256]{1,0:T(8,128)} %d_hbm.1) | copy-start | bytes 49156

commit v2 on v1

--- a/solution.py
+++ b/solution.py
@@ -11,6 +11,7 @@
 MESH = pl.DeviceIdType.MESH
 f32 = jnp.float32
 bf16 = jnp.bfloat16
+VMEM_LIMIT = 63 * 1024 * 1024
 LOG2E = math.log2(math.e)
 
 
@@ -42,14 +43,16 @@
 def row_operand(a):
     sq = 5.0 * jnp.sum(a * a, axis=0, keepdims=True)
     return jnp.concatenate(
-        [(-8.0 * a).astype(bf16), (-2.0 * a).astype(bf16), norm_tail(sq, False, 5.0)], axis=0
+        [(-8.0 * a).astype(bf16), (-2.0 * a).astype(bf16), norm_tail(sq, False, 5.0),
+         jnp.zeros((48, a.shape[1]), bf16)], axis=0
     )
 
 
 def col_operand(b):
     wide = b.astype(f32)
     sq = jnp.sum(wide * wide, axis=0, keepdims=True)
-    return jnp.concatenate([b, b, norm_tail(sq, True, 1.0)], axis=0)
+    fill = jnp.zeros((48, b.shape[1]), bf16)
+    return jnp.concatenate([b, b, norm_tail(sq, True, 1.0), fill], axis=0).T
 
 
 def matern(v):
@@ -166,9 +169,7 @@
         d_low = b_all[src, 32:48, :]
         both = b_all[src, 32:64, :]
         for t in range(C + tiles):
-            v = lax.dot_general(
-                b_op, a_op[t], (((0,), (0,)), ((), ())), preferred_element_type=f32
-            )
+            v = jnp.dot(b_op, a_op[t], preferred_element_type=f32)
             kern = matern(v)
             if t < C:
                 part[t] += jnp.dot(d_low, kern, preferred_element_type=f32)
@@ -246,6 +247,15 @@
         copy.wait_send()
 
 
+def hand_over(*refs):
+    sem = refs[8]
+    copies = [pltpu.make_async_copy(refs[i], refs[4 + i], sem.at[i]) for i in range(4)]
+    for copy in copies:
+        copy.start()
+    for copy in copies:
+        copy.wait()
+
+
 def per_device(R, C, points, candidates, length_scales, signal_var, noise_var, cand_prior, weights, residual, direction):
     F, L = points.shape
     Q = candidates.shape[1]
@@ -256,9 +266,10 @@
     vmem = pl.BlockSpec(memory_space=pltpu.VMEM)
     dma = pltpu.SemaphoreType.DMA
     state = jax.ShapeDtypeStruct((cols, L), f32)
-    return pl.pallas_call(
+    shapes = (state, state, state, jax.ShapeDtypeStruct((cols, Q), f32))
+    results = pl.pallas_call(
         functools.partial(kernel, R, C),
-        out_shape=(state, state, state, jax.ShapeDtypeStruct((cols, Q), f32)),
+        out_shape=shapes,
         in_specs=[hbm, hbm, hbm, smem, smem, hbm, hbm, hbm, hbm],
         out_specs=(vmem, vmem, vmem, vmem),
         scratch_shapes=[
@@ -272,7 +283,7 @@
             pltpu.VMEM((R, F + 2 * cols, L), bf16),
             pltpu.VMEM((C, F, L), bf16),
             pltpu.VMEM((C, F, Q), bf16),
-            pltpu.VMEM((C + tiles, 2 * F + 16, L), bf16),
+            pltpu.VMEM((C + tiles, 128, L), bf16),
             pltpu.VMEM((C, cols, L), f32),
             pltpu.VMEM((C, cols, L), f32),
             pltpu.VMEM((tiles, 2 * cols, L), f32),
@@ -290,12 +301,20 @@
             dma((R,)), dma((R,)),
         ],
         compiler_params=pltpu.CompilerParams(
-            collective_id=0, has_side_effects=True, vmem_limit_bytes=48 * 1024 * 1024
+            collective_id=0, has_side_effects=True, vmem_limit_bytes=VMEM_LIMIT
         ),
     )(
         points, candidates, length_scales[None, :], signal_var, noise_var,
         cand_prior[None, :], weights, residual, direction,
     )
+    return pl.pallas_call(
+        hand_over,
+        out_shape=shapes,
+        in_specs=[hbm] * 4,
+        out_specs=(hbm,) * 4,
+        scratch_shapes=[dma((4,))],
+        compiler_params=pltpu.CompilerParams(vmem_limit_bytes=VMEM_LIMIT),
+    )(*results)
 
 
 def solution(mesh):

time: 37.4 us -> 34.2 us (0.914)
  local copies, waits for them, and re-layouts: 6.7 us -> 0 us
  Pallas kernels: 28.2 us -> 32.1 us
    unnamed x18 -> x0, local copies, waits for them, and re-layouts: 6.7 us -> none
    pallas_call x1 -> x2, Pallas kernels: 28.2 us -> 32.1 us  [the longest x1 29.2 us: per_device(): pl.pallas_call(functools.partial(kernel, R, C), out_shape=shapes, in_spec...]
where the time goes in v2:
time: 34.2 us; the launch traced here: 34 us
  Pallas kernels  32.1 us (94%)
  between operations  1.93 us (6%)
    pallas_call x1, Pallas kernels, per_device(): pl.pallas_call(functools.partial(kernel, R, C), out_shape=shapes, in_spec...  29.2 us
    pallas_call x1, Pallas kernels, per_device(): pl.pallas_call(hand_over, out_shape=shapes, in_specs=[hbm] * 4, out_specs...  2.88 us

profile of v2, /device:TPU:0, one launch (start us, length us, event | category | flops | bytes accessed | tf_op | source)
XLA Modules:
  0.0 34.0 jit_solution(3218421939212939917)
XLA Ops:
  1.9 29.2 %shard_map.120 = (f32[16,256]{1,0:T(8,128)}, f32[16,256]{1,0:T(8,128)}, f32[16,256]{1,0:T(8,128)}, f32[16,64]{1,0:T(8,128)}) custom-call(f32[32,256]{1,0:T(8,128)} %pts_hbm.1, f32[32,64]{1,0:T(8,128)} %cand_hbm.1, f32[1,32]{1,0:T(1,128)} %bitcast.2, f32[1]{0:T(128)S(6)} %copy.13.sig_ref, f32[1]{0:T(128)S(6)} %copy.14.noise_ref, f32[1,64]{1,0:T(1,128)} %bitcast.3, ...), custom_call_target="tpu_custom_call" | custom-call | tf_op jit(solution)/shard_map/pallas_call | solution.py:270
  31.1 2.9 %shard_map.121 = (f32[16,256]{1,0:T(8,128)}, f32[16,256]{1,0:T(8,128)}, f32[16,256]{1,0:T(8,128)}, f32[16,64]{1,0:T(8,128)}) custom-call(f32[16,256]{1,0:T(8,128)} %get-tuple-element.8.refs_0_, f32[16,256]{1,0:T(8,128)} %get-tuple-element.9.refs_1_, f32[16,256]{1,0:T(8,128)} %get-tuple-element.10.refs_2_, f32[16,64]{1,0:T(8,128)} %get-tuple-element.11.refs_3_), custom_call_target="tpu_custom_call" | custom-call | tf_op jit(solution)/shard_map/pallas_call | solution.py:310

commit v3 on v2

--- a/solution.py
+++ b/solution.py
@@ -66,9 +66,9 @@
     pts_hbm, cand_hbm, ls_hbm, sig_ref, noise_ref, prior_hbm, w_hbm, r_hbm, d_hbm,
     wn_ref, rn_ref, dn_ref, cf_ref,
     pts_v, cand_v, ls_v, prior_v, w_v, r_v, d_v,
-    b_all, a_pts, a_cand, a_op, part, part_in, cpart, cout, cin, st_a, st_b,
+    b_all, a_pts, a_cand, a_op, part, part_in, cpart, cout, cin, st,
     in_sem, b_send, b_recv, a_send, a_recv, c_send, c_recv,
-    p_send, p_recv, q_send, q_recv, s_send, s_recv, t_send, t_recv,
+    p_send, p_recv, q_send, q_recv, s_send, s_recv,
 ):
     row = lax.axis_index("row")
     col = lax.axis_index("col")
@@ -86,10 +86,13 @@
         copy.start()
 
     barrier = pltpu.get_barrier_semaphore()
-    for k in range(1, C):
-        pl.semaphore_signal(barrier, inc=1, device_id=(row, flip(col, k, C)), device_id_type=MESH)
-    for k in range(1, R):
-        pl.semaphore_signal(barrier, inc=1, device_id=(flip(row, k, R), col), device_id_type=MESH)
+    def greet(k, carry):
+        pl.semaphore_signal(
+            barrier, inc=1, device_id=(flip(row, k // C, R), flip(col, k % C, C)), device_id_type=MESH
+        )
+        return carry
+
+    lax.fori_loop(1, R * C, greet, 0)
 
     def col_copy(k, src, dst, send, recv):
         peer = flip(col, k, C)
@@ -132,27 +135,45 @@
     b_all[row, 32:48, :] = d_v[...].astype(bf16)
     b_all[row, 48:64, :] = w_v[...].astype(bf16)
 
-    pl.semaphore_wait(barrier, C - 1 + R - 1)
+    pl.semaphore_wait(barrier, R * C - 1)
     sends = []
     for k in range(1, C):
         sends.append(col_copy(k, a_pts.at[col], a_pts, a_send, a_recv))
         sends[-1].start()
         sends.append(col_copy(k, a_cand.at[col], a_cand, c_send, c_recv))
         sends[-1].start()
-    for k in range(1, R):
+    direct = list(range(2, R, 2)) + [1]
+    for k in direct:
         sends.append(row_copy(k, b_all.at[row], b_all, b_send, b_recv))
         sends[-1].start()
 
     part[...] = jnp.zeros_like(part)
     cpart[...] = jnp.zeros_like(cpart)
 
-    for k in range(1, C):
-        col_arrive(k, a_pts, a_recv)
-        col_arrive(k, a_cand, c_recv)
-    for k in range(C):
-        a_op[k] = row_operand(a_pts[k].astype(f32))
     per_tile = L // Q
     tiles = C // per_tile
+
+    def prepare(src):
+        return col_operand(b_all[src, 0:32, :]), b_all[src, 32:48, :], b_all[src, 32:64, :]
+
+    def run_tile(t, chunk):
+        kern = matern(jnp.dot(chunk[0], a_op[t], preferred_element_type=f32))
+        part[t] += jnp.dot(chunk[1], kern, preferred_element_type=f32)
+
+    def cand_tile(t, chunk):
+        kern = matern(jnp.dot(chunk[0], a_op[C + t], preferred_element_type=f32))
+        cpart[t] += jnp.dot(chunk[2], kern, preferred_element_type=f32)
+
+    own = prepare(row)
+    a_op[col] = row_operand(a_pts[col].astype(f32))
+    run_tile(col, own)
+    for k in range(1, C):
+        peer = flip(col, k, C)
+        col_arrive(k, a_pts, a_recv)
+        a_op[peer] = row_operand(a_pts[peer].astype(f32))
+        run_tile(peer, own)
+    for k in range(1, C):
+        col_arrive(k, a_cand, c_recv)
     for t in range(tiles):
         wide = None
         for k in range(per_tile):
@@ -163,37 +184,60 @@
             term = jnp.dot(a_cand[t * per_tile + k], place, preferred_element_type=f32)
             wide = term if wide is None else wide + term
         a_op[C + t] = row_operand(wide)
-
-    def chunk(src):
-        b_op = col_operand(b_all[src, 0:32, :])
-        d_low = b_all[src, 32:48, :]
-        both = b_all[src, 32:64, :]
-        for t in range(C + tiles):
-            v = jnp.dot(b_op, a_op[t], preferred_element_type=f32)
-            kern = matern(v)
-            if t < C:
-                part[t] += jnp.dot(d_low, kern, preferred_element_type=f32)
-            else:
-                cpart[t - C] += jnp.dot(both, kern, preferred_element_type=f32)
-
-    chunk(row)
-
-    def step(k, carry):
+        cand_tile(t, own)
+
+    def whole_chunk(k):
+        chunk = prepare(flip(row, k, R))
+        for t in range(C):
+            run_tile(t, chunk)
+        for t in range(tiles):
+            cand_tile(t, chunk)
+
+    def forward(k):
+        src = flip(row, k, R)
+        return pltpu.make_async_remote_copy(
+            src_ref=b_all.at[src], dst_ref=b_all.at[src], send_sem=b_send.at[k + 1],
+            recv_sem=b_recv.at[src], device_id=(flip(row, 1, R), col), device_id_type=MESH,
+        )
+
+    def step_direct(i, carry):
+        k = 2 * i
         row_arrive(k, b_all, b_recv)
-        chunk(flip(row, k, R))
-        return carry
-
-    lax.fori_loop(1, R, step, 0)
-
-    for k in range(1, C):
-        sends.append(col_copy(k, part.at[flip(col, k, C)], part_in, p_send, p_recv))
+        forward(k).start()
+        whole_chunk(k)
+        return carry
+
+    def step_forwarded(i, carry):
+        k = 2 * i + 1
+        row_arrive(k, b_all, b_recv)
+        whole_chunk(k)
+        return carry
+
+    lax.fori_loop(1, R // 2, step_direct, 0)
+    lax.fori_loop(0, R // 2 - 2, step_forwarded, 0)
+    for k in range(2, R, 2):
+        sends.append(forward(k))
+
+    last = []
+    for k in (R - 3, R - 1):
+        row_arrive(k, b_all, b_recv)
+        last.append(prepare(flip(row, k, R)))
+    for k in range(C - 1, 0, -1):
+        peer = flip(col, k, C)
+        for chunk in last:
+            run_tile(peer, chunk)
+        sends.append(col_copy(k, part.at[peer], part_in, p_send, p_recv))
         sends[-1].start()
     for t in range(tiles):
+        for chunk in last:
+            cand_tile(t, chunk)
         for k in range(per_tile):
             cout[t * per_tile + k] = cpart[t, :, k * Q:(k + 1) * Q]
     for k in range(1, C):
         sends.append(col_copy(k, cout.at[flip(col, k, C)], cin, q_send, q_recv))
         sends[-1].start()
+    for chunk in last:
+        run_tile(col, chunk)
 
     signal = sig_ref[0]
     d = d_v[...]
@@ -212,25 +256,41 @@
         packed = packed + jnp.where(lane == sub + 16 * q, value, 0.0)
     packed = jnp.sum(packed, axis=0, keepdims=True)
 
-    st_a[col] = packed
-    for k in range(1, C):
-        sends.append(col_copy(k, st_a.at[col], st_a, s_send, s_recv))
-        sends[-1].start()
-    for k in range(1, C):
-        col_arrive(k, st_a, s_recv)
-    st_b[row] = jnp.sum(st_a[...], axis=0)
-    for k in range(1, R):
-        sends.append(row_copy(k, st_b.at[row], st_b, t_send, t_recv))
-        sends[-1].start()
+    me = row * C + col
+    st[me] = packed
+
+    def sums_copy(k):
+        return pltpu.make_async_remote_copy(
+            src_ref=st.at[me], dst_ref=st.at[me], send_sem=s_send.at[k], recv_sem=s_recv.at[me],
+            device_id=(flip(row, k // C, R), flip(col, k % C, C)), device_id_type=MESH,
+        )
+
+    def sums_start(k, carry):
+        sums_copy(k).start()
+        return carry
+
+    def sums_arrive(k, carry):
+        peer = flip(row, k // C, R) * C + flip(col, k % C, C)
+        pltpu.make_async_remote_copy(
+            src_ref=st.at[peer], dst_ref=st.at[peer], send_sem=s_recv.at[peer],
+            recv_sem=s_recv.at[peer],
+            device_id=(flip(row, k // C, R), flip(col, k % C, C)), device_id_type=MESH,
+        ).wait_recv()
+        return carry
+
+    def sums_sent(k, carry):
+        sums_copy(k).wait_send()
+        return carry
+
+    lax.fori_loop(1, R * C, sums_start, 0)
 
     fit = cout[col]
     for k in range(1, C):
         col_arrive(k, cin, q_recv)
         fit = fit + cin[flip(col, k, C)]
 
-    for k in range(1, R):
-        row_arrive(k, st_b, t_recv)
-    sums = jnp.broadcast_to(jnp.sum(st_b[...], axis=0), (16, 128))
+    lax.fori_loop(1, R * C, sums_arrive, 0)
+    sums = jnp.broadcast_to(jnp.sum(st[...], axis=0), (16, 128))
 
     def column(q):
         return jnp.sum(jnp.where(lane == sub + 16 * q, sums, 0.0), axis=1, keepdims=True)
@@ -245,15 +305,12 @@
     cf_ref[...] = prior_v[...] + signal * (fit[16:32] + step_len * fit[0:16])
     for copy in sends:
         copy.wait_send()
+    lax.fori_loop(1, R * C, sums_sent, 0)
 
 
 def hand_over(*refs):
-    sem = refs[8]
-    copies = [pltpu.make_async_copy(refs[i], refs[4 + i], sem.at[i]) for i in range(4)]
-    for copy in copies:
-        copy.start()
-    for copy in copies:
-        copy.wait()
+    for i in range(4):
+        refs[4 + i][...] = refs[i][...]
 
 
 def per_device(R, C, points, candidates, length_scales, signal_var, noise_var, cand_prior, weights, residual, direction):
@@ -289,16 +346,14 @@
             pltpu.VMEM((tiles, 2 * cols, L), f32),
             pltpu.VMEM((C, 2 * cols, Q), f32),
             pltpu.VMEM((C, 2 * cols, Q), f32),
-            pltpu.VMEM((C, 1, 128), f32),
-            pltpu.VMEM((R, 1, 128), f32),
+            pltpu.VMEM((R * C, 1, 128), f32),
             dma((7,)),
             dma((R,)), dma((R,)),
             dma((C,)), dma((C,)),
             dma((C,)), dma((C,)),
             dma((C,)), dma((C,)),
             dma((C,)), dma((C,)),
-            dma((C,)), dma((C,)),
-            dma((R,)), dma((R,)),
+            dma((R * C,)), dma((R * C,)),
         ],
         compiler_params=pltpu.CompilerParams(
             collective_id=0, has_side_effects=True, vmem_limit_bytes=VMEM_LIMIT
@@ -310,9 +365,8 @@
     return pl.pallas_call(
         hand_over,
         out_shape=shapes,
-        in_specs=[hbm] * 4,
-        out_specs=(hbm,) * 4,
-        scratch_shapes=[dma((4,))],
+        in_specs=[vmem] * 4,
+        out_specs=(vmem,) * 4,
         compiler_params=pltpu.CompilerParams(vmem_limit_bytes=VMEM_LIMIT),
     )(*results)
 

time: 34.2 us -> 31.2 us (0.912)
  Pallas kernels: 32.1 us -> 29.1 us
    pallas_call x1, Pallas kernels: 29.2 us -> 27.7 us  [per_device(): pl.pallas_call(functools.partial(kernel, R, C), out_shape=shapes, in_spec...]
    pallas_call x1, Pallas kernels: 2.88 us -> 1.38 us  [per_device(): pl.pallas_call(hand_over, out_shape=shapes, in_specs=[vmem] * 4, out_spec...]
where the time goes in v3:
time: 31.2 us; the launch traced here: 31 us
  Pallas kernels  29.1 us (93%)
  between operations  1.93 us (6%)
    pallas_call x1, Pallas kernels, per_device(): pl.pallas_call(functools.partial(kernel, R, C), out_shape=shapes, in_spec...  27.7 us
    pallas_call x1, Pallas kernels, per_device(): pl.pallas_call(hand_over, out_shape=shapes, in_specs=[vmem] * 4, out_spec...  1.38 us

profile of v3, /device:TPU:0, one launch (start us, length us, event | category | flops | bytes accessed | tf_op | source)
XLA Modules:
  0.0 31.0 jit_solution(12463021975991180471)
XLA Ops:
  1.9 27.7 %shard_map.120 = (f32[16,256]{1,0:T(8,128)}, f32[16,256]{1,0:T(8,128)}, f32[16,256]{1,0:T(8,128)}, f32[16,64]{1,0:T(8,128)}) custom-call(f32[32,256]{1,0:T(8,128)} %pts_hbm.1, f32[32,64]{1,0:T(8,128)} %cand_hbm.1, f32[1,32]{1,0:T(1,128)} %bitcast.2, f32[1]{0:T(128)S(6)} %copy.13.sig_ref, f32[1]{0:T(128)S(6)} %copy.14.noise_ref, f32[1,64]{1,0:T(1,128)} %bitcast.3, ...), custom_call_target="tpu_custom_call" | custom-call | tf_op jit(solution)/shard_map/pallas_call | solution.py:327
  29.6 1.4 %shard_map.121 = (f32[16,256]{1,0:T(8,128)}, f32[16,256]{1,0:T(8,128)}, f32[16,256]{1,0:T(8,128)}, f32[16,64]{1,0:T(8,128)}) custom-call(f32[16,256]{1,0:T(8,128)} %get-tuple-element.8.refs_0_, f32[16,256]{1,0:T(8,128)} %get-tuple-element.9.refs_1_, f32[16,256]{1,0:T(8,128)} %get-tuple-element.10.refs_2_, f32[16,64]{1,0:T(8,128)} %get-tuple-element.11.refs_3_), custom_call_target="tpu_custom_call" | custom-call | tf_op jit(solution)/shard_map/pallas_call | solution.py:365

commit v4 on v3

--- a/solution.py
+++ b/solution.py
@@ -11,6 +11,7 @@
 MESH = pl.DeviceIdType.MESH
 f32 = jnp.float32
 bf16 = jnp.bfloat16
+PIECE = 32
 VMEM_LIMIT = 63 * 1024 * 1024
 LOG2E = math.log2(math.e)
 
@@ -66,7 +67,7 @@
     pts_hbm, cand_hbm, ls_hbm, sig_ref, noise_ref, prior_hbm, w_hbm, r_hbm, d_hbm,
     wn_ref, rn_ref, dn_ref, cf_ref,
     pts_v, cand_v, ls_v, prior_v, w_v, r_v, d_v,
-    b_all, a_pts, a_cand, a_op, part, part_in, cpart, cout, cin, st,
+    b_all, a_pts, a_cand, a_op, v_buf, k_buf, acc, part_in, cout, cin, st,
     in_sem, b_send, b_recv, a_send, a_recv, c_send, c_recv,
     p_send, p_recv, q_send, q_recv, s_send, s_recv,
 ):
@@ -147,31 +148,43 @@
         sends.append(row_copy(k, b_all.at[row], b_all, b_send, b_recv))
         sends[-1].start()
 
-    part[...] = jnp.zeros_like(part)
-    cpart[...] = jnp.zeros_like(cpart)
+    acc[...] = jnp.zeros_like(acc)
 
     per_tile = L // Q
     tiles = C // per_tile
 
     def prepare(src):
-        return col_operand(b_all[src, 0:32, :]), b_all[src, 32:48, :], b_all[src, 32:64, :]
-
-    def run_tile(t, chunk):
-        kern = matern(jnp.dot(chunk[0], a_op[t], preferred_element_type=f32))
-        part[t] += jnp.dot(chunk[1], kern, preferred_element_type=f32)
-
-    def cand_tile(t, chunk):
-        kern = matern(jnp.dot(chunk[0], a_op[C + t], preferred_element_type=f32))
-        cpart[t] += jnp.dot(chunk[2], kern, preferred_element_type=f32)
+        return col_operand(b_all[src, 0:32, :]), b_all[src, 32:64, :]
+
+    def run(chunks, first, end):
+        jobs = [(t, i) for t in range(first, end) for i in range(len(chunks))]
+
+        def inner(n):
+            t, i = jobs[n]
+            v_buf[n % 4] = jnp.dot(
+                chunks[i][0], a_op[:, t * L:(t + 1) * L], preferred_element_type=f32
+            )
+
+        inner(0)
+        for n, (t, i) in enumerate(jobs):
+            if n + 1 < len(jobs):
+                inner(n + 1)
+            for p in range(0, L, PIECE):
+                k_buf[n % 4, p:p + PIECE, :] = matern(v_buf[n % 4, p:p + PIECE, :])
+            acc[:, t * L:(t + 1) * L] += jnp.dot(
+                chunks[i][1], k_buf[n % 4], preferred_element_type=f32
+            )
+
+    def slot(k):
+        start = (tiles + k) * L if k else 0
+        return slice(start, start + L)
 
     own = prepare(row)
-    a_op[col] = row_operand(a_pts[col].astype(f32))
-    run_tile(col, own)
-    for k in range(1, C):
-        peer = flip(col, k, C)
+    a_op[:, slot(0)] = row_operand(a_pts[col].astype(f32))
+    run([own], 0, 1)
+    for k in range(1, C):
         col_arrive(k, a_pts, a_recv)
-        a_op[peer] = row_operand(a_pts[peer].astype(f32))
-        run_tile(peer, own)
+        a_op[:, slot(k)] = row_operand(a_pts[flip(col, k, C)].astype(f32))
     for k in range(1, C):
         col_arrive(k, a_cand, c_recv)
     for t in range(tiles):
@@ -181,17 +194,15 @@
                 lax.broadcasted_iota(jnp.int32, (Q, L), 1)
                 == lax.broadcasted_iota(jnp.int32, (Q, L), 0) + k * Q
             ).astype(f32).astype(bf16)
-            term = jnp.dot(a_cand[t * per_tile + k], place, preferred_element_type=f32)
+            term = jnp.dot(
+                a_cand[flip(col, t * per_tile + k, C)], place, preferred_element_type=f32
+            )
             wide = term if wide is None else wide + term
-        a_op[C + t] = row_operand(wide)
-        cand_tile(t, own)
+        a_op[:, (1 + t) * L:(2 + t) * L] = row_operand(wide)
+    run([own], 1, C + tiles)
 
     def whole_chunk(k):
-        chunk = prepare(flip(row, k, R))
-        for t in range(C):
-            run_tile(t, chunk)
-        for t in range(tiles):
-            cand_tile(t, chunk)
+        run([prepare(flip(row, k, R))], 0, C + tiles)
 
     def forward(k):
         src = flip(row, k, R)
@@ -222,27 +233,21 @@
     for k in (R - 3, R - 1):
         row_arrive(k, b_all, b_recv)
         last.append(prepare(flip(row, k, R)))
+    run(last, 1 + tiles, C + tiles)
     for k in range(C - 1, 0, -1):
-        peer = flip(col, k, C)
-        for chunk in last:
-            run_tile(peer, chunk)
-        sends.append(col_copy(k, part.at[peer], part_in, p_send, p_recv))
-        sends[-1].start()
-    for t in range(tiles):
-        for chunk in last:
-            cand_tile(t, chunk)
-        for k in range(per_tile):
-            cout[t * per_tile + k] = cpart[t, :, k * Q:(k + 1) * Q]
-    for k in range(1, C):
-        sends.append(col_copy(k, cout.at[flip(col, k, C)], cin, q_send, q_recv))
-        sends[-1].start()
-    for chunk in last:
-        run_tile(col, chunk)
+        sends.append(col_copy(k, acc.at[0:16, slot(k)], part_in, p_send, p_recv))
+        sends[-1].start()
+    run(last, 0, 1 + tiles)
+    for k in range(C):
+        cout[k] = acc[:, L + k * Q:L + (k + 1) * Q]
+    for k in range(1, C):
+        sends.append(col_copy(k, cout.at[k], cin, q_send, q_recv))
+        sends[-1].start()
 
     signal = sig_ref[0]
     d = d_v[...]
     r = r_v[...]
-    total = part[col]
+    total = acc[0:16, slot(0)]
     for k in range(1, C):
         col_arrive(k, part_in, p_recv)
         total = total + part_in[flip(col, k, C)]
@@ -284,7 +289,7 @@
 
     lax.fori_loop(1, R * C, sums_start, 0)
 
-    fit = cout[col]
+    fit = cout[0]
     for k in range(1, C):
         col_arrive(k, cin, q_recv)
         fit = fit + cin[flip(col, k, C)]
@@ -340,10 +345,11 @@
             pltpu.VMEM((R, F + 2 * cols, L), bf16),
             pltpu.VMEM((C, F, L), bf16),
             pltpu.VMEM((C, F, Q), bf16),
-            pltpu.VMEM((C + tiles, 128, L), bf16),
+            pltpu.VMEM((128, (C + tiles) * L), bf16),
+            pltpu.VMEM((4, L, L), f32),
+            pltpu.VMEM((4, L, L), bf16),
+            pltpu.VMEM((2 * cols, (C + tiles) * L), f32),
             pltpu.VMEM((C, cols, L), f32),
-            pltpu.VMEM((C, cols, L), f32),
-            pltpu.VMEM((tiles, 2 * cols, L), f32),
             pltpu.VMEM((C, 2 * cols, Q), f32),
             pltpu.VMEM((C, 2 * cols, Q), f32),
             pltpu.VMEM((R * C, 1, 128), f32),

time: 31.2 us -> 30.6 us (0.981)
  Pallas kernels: 29.1 us -> 28.4 us
    pallas_call x1, Pallas kernels: 27.7 us -> 27.1 us  [per_device(): pl.pallas_call(functools.partial(kernel, R, C), out_shape=shapes, in_spec...]
where the time goes in v4:
time: 30.6 us; the launch traced here: 30.4 us
  Pallas kernels  28.4 us (93%)
  between operations  1.93 us (6%)
    pallas_call x1, Pallas kernels, per_device(): pl.pallas_call(functools.partial(kernel, R, C), out_shape=shapes, in_spec...  27.1 us
    pallas_call x1, Pallas kernels, per_device(): pl.pallas_call(hand_over, out_shape=shapes, in_specs=[vmem] * 4, out_spec...  1.38 us

profile of v4, /device:TPU:0, one launch (start us, length us, event | category | flops | bytes accessed | tf_op | source)
XLA Modules:
  0.0 30.4 jit_solution(5543314720331742204)
XLA Ops:
  1.9 27.1 %shard_map.120 = (f32[16,256]{1,0:T(8,128)}, f32[16,256]{1,0:T(8,128)}, f32[16,256]{1,0:T(8,128)}, f32[16,64]{1,0:T(8,128)}) custom-call(f32[32,256]{1,0:T(8,128)} %pts_hbm.1, f32[32,64]{1,0:T(8,128)} %cand_hbm.1, f32[1,32]{1,0:T(1,128)} %bitcast.2, f32[1]{0:T(128)S(6)} %copy.13.sig_ref, f32[1]{0:T(128)S(6)} %copy.14.noise_ref, f32[1,64]{1,0:T(1,128)} %bitcast.3, ...), custom_call_target="tpu_custom_call" | custom-call | tf_op jit(solution)/shard_map/pallas_call | solution.py:332
  29.0 1.4 %shard_map.121 = (f32[16,256]{1,0:T(8,128)}, f32[16,256]{1,0:T(8,128)}, f32[16,256]{1,0:T(8,128)}, f32[16,64]{1,0:T(8,128)}) custom-call(f32[16,256]{1,0:T(8,128)} %get-tuple-element.8.refs_0_, f32[16,256]{1,0:T(8,128)} %get-tuple-element.9.refs_1_, f32[16,256]{1,0:T(8,128)} %get-tuple-element.10.refs_2_, f32[16,64]{1,0:T(8,128)} %get-tuple-element.11.refs_3_), custom_call_target="tpu_custom_call" | custom-call | tf_op jit(solution)/shard_map/pallas_call | solution.py:371

commit v5 on v4

--- a/solution.py
+++ b/solution.py
@@ -75,6 +75,11 @@
     col = lax.axis_index("col")
     L = pts_v.shape[1]
     Q = cand_v.shape[1]
+    row_peer = [flip(row, k, R) for k in range(R)]
+    col_peer = [flip(col, k, C) for k in range(C)]
+
+    def row_of(k):
+        return row_peer[k] if isinstance(k, int) else flip(row, k, R)
 
     loads = [
         pltpu.make_async_copy(src, dst, in_sem.at[i])
@@ -87,37 +92,45 @@
         copy.start()
 
     barrier = pltpu.get_barrier_semaphore()
-    def greet(k, carry):
-        pl.semaphore_signal(
-            barrier, inc=1, device_id=(flip(row, k // C, R), flip(col, k % C, C)), device_id_type=MESH
-        )
-        return carry
-
-    lax.fori_loop(1, R * C, greet, 0)
+    def everyone(visit):
+        for b in range(1, C):
+            visit(row, col_peer[b], b)
+
+        def turn(a, carry):
+            there = lax.rem(row + a, R)
+            for b in range(C):
+                visit(there, col_peer[b], a * C + b)
+            return carry
+
+        lax.fori_loop(1, R, turn, 0)
+
+    everyone(lambda r, c, k: pl.semaphore_signal(
+        barrier, inc=1, device_id=(r, c), device_id_type=MESH
+    ))
 
     def col_copy(k, src, dst, send, recv):
-        peer = flip(col, k, C)
+        peer = col_peer[k]
         return pltpu.make_async_remote_copy(
             src_ref=src, dst_ref=dst.at[col], send_sem=send.at[k], recv_sem=recv.at[col],
             device_id=(row, peer), device_id_type=MESH,
         )
 
     def col_arrive(k, dst, recv):
-        peer = flip(col, k, C)
+        peer = col_peer[k]
         pltpu.make_async_remote_copy(
             src_ref=dst.at[peer], dst_ref=dst.at[peer], send_sem=recv.at[peer],
             recv_sem=recv.at[peer], device_id=(row, peer), device_id_type=MESH,
         ).wait_recv()
 
     def row_copy(k, src, dst, send, recv):
-        peer = flip(row, k, R)
+        peer = row_of(k)
         return pltpu.make_async_remote_copy(
             src_ref=src, dst_ref=dst.at[row], send_sem=send.at[k], recv_sem=recv.at[row],
             device_id=(peer, col), device_id_type=MESH,
         )
 
     def row_arrive(k, dst, recv):
-        peer = flip(row, k, R)
+        peer = row_of(k)
         pltpu.make_async_remote_copy(
             src_ref=dst.at[peer], dst_ref=dst.at[peer], send_sem=recv.at[peer],
             recv_sem=recv.at[peer], device_id=(peer, col), device_id_type=MESH,
@@ -184,7 +197,7 @@
     run([own], 0, 1)
     for k in range(1, C):
         col_arrive(k, a_pts, a_recv)
-        a_op[:, slot(k)] = row_operand(a_pts[flip(col, k, C)].astype(f32))
+        a_op[:, slot(k)] = row_operand(a_pts[col_peer[k]].astype(f32))
     for k in range(1, C):
         col_arrive(k, a_cand, c_recv)
     for t in range(tiles):
@@ -195,20 +208,20 @@
                 == lax.broadcasted_iota(jnp.int32, (Q, L), 0) + k * Q
             ).astype(f32).astype(bf16)
             term = jnp.dot(
-                a_cand[flip(col, t * per_tile + k, C)], place, preferred_element_type=f32
+                a_cand[col_peer[t * per_tile + k]], place, preferred_element_type=f32
             )
             wide = term if wide is None else wide + term
         a_op[:, (1 + t) * L:(2 + t) * L] = row_operand(wide)
     run([own], 1, C + tiles)
 
     def whole_chunk(k):
-        run([prepare(flip(row, k, R))], 0, C + tiles)
+        run([prepare(row_of(k))], 0, C + tiles)
 
     def forward(k):
-        src = flip(row, k, R)
+        src = row_of(k)
         return pltpu.make_async_remote_copy(
             src_ref=b_all.at[src], dst_ref=b_all.at[src], send_sem=b_send.at[k + 1],
-            recv_sem=b_recv.at[src], device_id=(flip(row, 1, R), col), device_id_type=MESH,
+            recv_sem=b_recv.at[src], device_id=(row_peer[1], col), device_id_type=MESH,
         )
 
     def step_direct(i, carry):
@@ -232,7 +245,7 @@
     last = []
     for k in (R - 3, R - 1):
         row_arrive(k, b_all, b_recv)
-        last.append(prepare(flip(row, k, R)))
+        last.append(prepare(row_of(k)))
     run(last, 1 + tiles, C + tiles)
     for k in range(C - 1, 0, -1):
         sends.append(col_copy(k, acc.at[0:16, slot(k)], part_in, p_send, p_recv))
@@ -250,7 +263,7 @@
     total = acc[0:16, slot(0)]
     for k in range(1, C):
         col_arrive(k, part_in, p_recv)
-        total = total + part_in[flip(col, k, C)]
+        total = total + part_in[col_peer[k]]
     image = signal * total + noise_ref[0] * d
 
     lane = lax.broadcasted_iota(jnp.int32, (16, 128), 1)
@@ -264,37 +277,27 @@
     me = row * C + col
     st[me] = packed
 
-    def sums_copy(k):
+    def sums_copy(r, c, k):
         return pltpu.make_async_remote_copy(
             src_ref=st.at[me], dst_ref=st.at[me], send_sem=s_send.at[k], recv_sem=s_recv.at[me],
-            device_id=(flip(row, k // C, R), flip(col, k % C, C)), device_id_type=MESH,
-        )
-
-    def sums_start(k, carry):
-        sums_copy(k).start()
-        return carry
-
-    def sums_arrive(k, carry):
-        peer = flip(row, k // C, R) * C + flip(col, k % C, C)
+            device_id=(r, c), device_id_type=MESH,
+        )
+
+    def sums_arrive(r, c, k):
+        peer = r * C + c
         pltpu.make_async_remote_copy(
             src_ref=st.at[peer], dst_ref=st.at[peer], send_sem=s_recv.at[peer],
-            recv_sem=s_recv.at[peer],
-            device_id=(flip(row, k // C, R), flip(col, k % C, C)), device_id_type=MESH,
+            recv_sem=s_recv.at[peer], device_id=(r, c), device_id_type=MESH,
         ).wait_recv()
-        return carry
-
-    def sums_sent(k, carry):
-        sums_copy(k).wait_send()
-        return carry
-
-    lax.fori_loop(1, R * C, sums_start, 0)
+
+    everyone(lambda r, c, k: sums_copy(r, c, k).start())
 
     fit = cout[0]
     for k in range(1, C):
         col_arrive(k, cin, q_recv)
-        fit = fit + cin[flip(col, k, C)]
-
-    lax.fori_loop(1, R * C, sums_arrive, 0)
+        fit = fit + cin[col_peer[k]]
+
+    everyone(sums_arrive)
     sums = jnp.broadcast_to(jnp.sum(st[...], axis=0), (16, 128))
 
     def column(q):
@@ -310,7 +313,7 @@
     cf_ref[...] = prior_v[...] + signal * (fit[16:32] + step_len * fit[0:16])
     for copy in sends:
         copy.wait_send()
-    lax.fori_loop(1, R * C, sums_sent, 0)
+    everyone(lambda r, c, k: sums_copy(r, c, k).wait_send())
 
 
 def hand_over(*refs):

time: 30.6 us -> 28.7 us (0.938)
  Pallas kernels: 28.4 us -> 26.5 us
    pallas_call x1, Pallas kernels: 27.1 us -> 25.1 us  [per_device(): pl.pallas_call(functools.partial(kernel, R, C), out_shape=shapes, in_spec...]
where the time goes in v5:
time: 28.7 us; the launch traced here: 28.4 us
  Pallas kernels  26.5 us (92%)
  between operations  1.93 us (7%)
    pallas_call x1, Pallas kernels, per_device(): pl.pallas_call(functools.partial(kernel, R, C), out_shape=shapes, in_spec...  25.1 us
    pallas_call x1, Pallas kernels, per_device(): pl.pallas_call(hand_over, out_shape=shapes, in_specs=[vmem] * 4, out_spec...  1.38 us

profile of v5, /device:TPU:0, one launch (start us, length us, event | category | flops | bytes accessed | tf_op | source)
XLA Modules:
  0.0 28.4 jit_solution(16581361061619774912)
XLA Ops:
  1.9 25.1 %shard_map.120 = (f32[16,256]{1,0:T(8,128)}, f32[16,256]{1,0:T(8,128)}, f32[16,256]{1,0:T(8,128)}, f32[16,64]{1,0:T(8,128)}) custom-call(f32[32,256]{1,0:T(8,128)} %pts_hbm.1, f32[32,64]{1,0:T(8,128)} %cand_hbm.1, f32[1,32]{1,0:T(1,128)} %bitcast.2, f32[1]{0:T(128)S(6)} %copy.13.sig_ref, f32[1]{0:T(128)S(6)} %copy.14.noise_ref, f32[1,64]{1,0:T(1,128)} %bitcast.3, ...), custom_call_target="tpu_custom_call" | custom-call | tf_op jit(solution)/shard_map/pallas_call | solution.py:335
  27.0 1.4 %shard_map.121 = (f32[16,256]{1,0:T(8,128)}, f32[16,256]{1,0:T(8,128)}, f32[16,256]{1,0:T(8,128)}, f32[16,64]{1,0:T(8,128)}) custom-call(f32[16,256]{1,0:T(8,128)} %get-tuple-element.8.refs_0_, f32[16,256]{1,0:T(8,128)} %get-tuple-element.9.refs_1_, f32[16,256]{1,0:T(8,128)} %get-tuple-element.10.refs_2_, f32[16,64]{1,0:T(8,128)} %get-tuple-element.11.refs_3_), custom_call_target="tpu_custom_call" | custom-call | tf_op jit(solution)/shard_map/pallas_call | solution.py:374
